TPU v7x, 32 devices: a whole 2x2x4 slice. The times are simulated.
32 devices in a mesh: group: 2 (over x), dp: 8 (over z, y), mp: 2 (over core).
Axes of the slice: x: 2, y: 2, z: 4, core: 2. Of those that a mesh axis runs over, the one named last changes fastest.
Arguments:
- input_tiles: bfloat16 [24576, 4096], P(('group', 'dp'), 'mp'), parts along dimension 0, may hold values from -6 to 6
- value_matrix: bfloat16 [4096, 1024], P('mp', 'dp'), may hold values from -0.09375 to 0.09375
- adapter_down_weight: bfloat16 [32, 4096, 32], P(('group', 'dp'), 'mp'), parts along dimension 0, may hold values from -0.09375 to 0.09375
- adapter_up_weight: bfloat16 [32, 32, 1024], P(('group', 'dp'), None, 'mp'), parts along dimension 0, may hold values from -1 to 1
- output_gradient: bfloat16 [24576, 1024], P(('group', 'dp'), 'mp'), parts along dimension 0, may hold values from -3 to 3
- tile_slot_target: int32 [192], P('group'), parts along dimension 0, may hold values from -1 to 95, as said below
- tile_owner_tenant: int32 [192], P('group'), parts along dimension 0, may hold values from 0 to 15, as said below
- tenant_storage_row: int32 [32], P('group'), parts along dimension 0, may hold values from 0 to 15, as said below
Outputs:
- moved_out: bfloat16 [24576, 1024], P(('group', 'dp'), 'mp'), parts along dimension 0
- grad_a: float32 [32, 4096, 32], P(('group', 'dp'), 'mp'), parts along dimension 0
- grad_b: float32 [32, 32, 1024], P(('group', 'dp'), None, 'mp'), parts along dimension 0
There are 2 independent parts, one for each index of `group`. A program takes and returns all parts, laid end to end along the dimension named above; an argument that names none is the same for every part. Nothing has to cross between parts.
Inputs may be any that keep to these rules, and one draw needn't show every extreme that they name: `tile_slot_target`: tile r * 12 + j sits on rank r of dp and goes to rank tile_target_i // 12; -1 means the tile is dropped; no slot is named twice; at most 2 tiles of one rank go to one rank, and some pair of ranks reaches 2; in every draw some rank receives 12 tiles. `tile_owner_tenant`: at most 2 tiles of one rank have tenants whose storage rows belong to one owner rank, and some rank reaches 2. `tenant_storage_row`: a permutation; storage row p belongs to rank p // 2 of dp.
All inputs are finite; a program needn't handle non-finite values.
Results may differ from a plain program's by a relative error of at most 0.0051.
Values may be sent and summed in bfloat16 or wider, within the bound.
A program may use at most 128 MiB of HBM per device.

v0:
```python
import jax
import jax.numpy as jnp
from jax import lax
from jax.sharding import PartitionSpec as P

ROWS = 128


adapter_scale = 0.25


def on_device(
    input_tiles,
    value_matrix,
    adapter_down_weight,
    adapter_up_weight,
    output_gradient,
    tile_slot_target,
    tile_owner_tenant,
    tenant_storage_row,
):
    single_tile = jnp.float32
    narrow_output = jnp.bfloat16
    ranks = lax.axis_size("dp")
    my_rank = lax.axis_index("dp")
    tile_rows = ROWS
    per_rank = input_tiles.shape[0] // tile_rows
    slot_count = output_gradient.shape[0] // tile_rows
    owned_adapters = adapter_down_weight.shape[0]
    half_cols = output_gradient.shape[1]
    feature_half = input_tiles.shape[1]
    level_list = (per_rank + ranks - 1) // ranks
    rank_ids = jnp.arange(ranks, dtype=jnp.int32)
    level_ids = jnp.arange(level_list, dtype=jnp.int32)
    storage_rows = tenant_storage_row[tile_owner_tenant].reshape(ranks, per_rank)
    owners = storage_rows // owned_adapters
    local_rows = storage_rows % owned_adapters
    targets = tile_slot_target.reshape(ranks, per_rank)
    dests = jnp.where(targets >= 0, targets // slot_count, -1)
    positions = jnp.arange(per_rank, dtype=jnp.int32)
    earlier = positions[:, None] < positions[None, :]

    def level_of(labels):
        matching = labels[:, :, None] == labels[:, None, :]
        found = jnp.sum((matching & earlier[None]).astype(jnp.int32), axis=1)
        return jnp.minimum(found, level_list - 1)

    owner_level = level_of(owners)
    dest_level = level_of(dests)
    serves = (
        (owners == my_rank)[:, :, None, None]
        & (owner_level[:, :, None, None] == level_ids[None, None, :, None])
        & (
            local_rows[:, :, None, None]
            == jnp.arange(owned_adapters, dtype=jnp.int32)[None, None, None, :]
        )
    )
    serving_tenants = jnp.sum(serves.astype(jnp.int32), axis=1).astype(narrow_output)
    slot_ids = my_rank * slot_count + jnp.arange(slot_count, dtype=jnp.int32)
    arrived = (targets[:, :, None, None] == slot_ids[None, None, None, :]) & (
        dest_level[:, :, None, None] == level_ids[None, None, :, None]
    )
    incoming = jnp.sum(arrived.astype(jnp.int32), axis=1).astype(narrow_output)
    my_owner = owners[my_rank]
    my_owner_level = owner_level[my_rank]
    my_dest = dests[my_rank]
    my_dest_level = dest_level[my_rank]
    my_places = storage_rows[my_rank]
    survives = my_dest >= 0
    grad_slots = output_gradient.reshape(slot_count, tile_rows, half_cols)
    send_grad = jnp.einsum(
        "rls,sbk->rlbk", incoming, grad_slots, preferred_element_type=single_tile
    ).astype(narrow_output)
    pieces = (
        lax.all_gather(adapter_down_weight, "dp", axis=0, tiled=True),
        lax.all_gather(adapter_up_weight, "dp", axis=0, tiled=True),
    )
    stored = jnp.arange(pieces[0].shape[0], dtype=jnp.int32)
    chosen = (my_places[:, None] == stored[None, :]).astype(narrow_output)
    part_down = jnp.einsum(
        "jp,pdq->jdq", chosen, pieces[0], preferred_element_type=single_tile
    ).astype(narrow_output)
    part_up = jnp.einsum(
        "jp,pqk->jqk", chosen, pieces[1], preferred_element_type=single_tile
    ).astype(narrow_output)
    recv_grad = lax.all_to_all(send_grad, "dp", split_axis=0, concat_axis=0, tiled=True)
    tile_stack = input_tiles.reshape(per_rank, tile_rows, feature_half)
    part_proj = jnp.dot(
        input_tiles,
        lax.all_gather(value_matrix, "dp", axis=1, tiled=True),
        preferred_element_type=single_tile,
    )
    part_low = jnp.einsum("tbd,tdq->tbq", tile_stack, part_down, preferred_element_type=single_tile)
    projected_rows = lax.psum_scatter(part_proj, "mp", scatter_dimension=1, tiled=True)
    reduced_activation = lax.psum(part_low, "mp")
    projected_rows = projected_rows.reshape(per_rank, tile_rows, half_cols)
    reduced_bfloat = reduced_activation.astype(narrow_output)
    output_half = (
        projected_rows
        + adapter_scale
        * jnp.einsum("yel,yls->yes", reduced_bfloat, part_up, preferred_element_type=single_tile)
    ).astype(narrow_output)
    to_dest = (
        (my_dest[None, None, :] == rank_ids[:, None, None])
        & (my_dest_level[None, None, :] == level_ids[None, :, None])
    ).astype(narrow_output)
    send_rows = jnp.einsum(
        "rlj,jbk->rlbk", to_dest, output_half, preferred_element_type=single_tile
    ).astype(narrow_output)
    recv_rows = lax.all_to_all(send_rows, "dp", split_axis=0, concat_axis=0, tiled=True)
    moved_out = jnp.einsum(
        "rls,rlbk->sbk", incoming, recv_rows, preferred_element_type=single_tile
    ).astype(narrow_output)
    moved_out = moved_out.reshape(slot_count * tile_rows, half_cols)
    gradient_portion = recv_grad[jnp.maximum(my_dest, 0), my_dest_level]
    gradient_portion = jnp.where(
        survives[:, None, None], gradient_portion, jnp.zeros((), narrow_output)
    )
    part_back = jnp.einsum(
        "tbk,tqk->tbq", gradient_portion, part_up, preferred_element_type=single_tile
    )
    reduced_gradient = lax.psum(part_back, "mp")
    reduced_gradient_bfloat = (adapter_scale * reduced_gradient).astype(narrow_output)
    down_term = jnp.einsum(
        "tbd,tbq->tdq", tile_stack, reduced_gradient_bfloat, preferred_element_type=single_tile
    ).astype(narrow_output)
    up_term = (
        adapter_scale
        * jnp.einsum(
            "uhz,uha->uza", reduced_bfloat, gradient_portion, preferred_element_type=single_tile
        )
    ).astype(narrow_output)
    to_owner = (
        (my_owner[None, None, :] == rank_ids[:, None, None])
        & (my_owner_level[None, None, :] == level_ids[None, :, None])
    ).astype(narrow_output)
    send_down_term = jnp.einsum(
        "rlj,jdq->rldq", to_owner, down_term, preferred_element_type=single_tile
    ).astype(narrow_output)
    send_up_term = jnp.einsum(
        "rlj,jqk->rlqk", to_owner, up_term, preferred_element_type=single_tile
    ).astype(narrow_output)
    recv_down_term, recv_up_term = (
        lax.all_to_all(send_down_term, "dp", split_axis=0, concat_axis=0, tiled=True),
        lax.all_to_all(send_up_term, "dp", split_axis=0, concat_axis=0, tiled=True),
    )
    grad_a = jnp.einsum(
        "rlt,rldq->tdq", serving_tenants, recv_down_term, preferred_element_type=single_tile
    )
    grad_b = jnp.einsum(
        "rlt,rlqk->tqk", serving_tenants, recv_up_term, preferred_element_type=single_tile
    )
    return (moved_out, grad_a, grad_b)


def solution(mesh):
    return jax.shard_map(
        on_device,
        mesh=mesh,
        in_specs=(
            P(("group", "dp"), "mp"),
            P("mp", "dp"),
            P(("group", "dp"), "mp", None),
            P(("group", "dp"), None, "mp"),
            P(("group", "dp"), "mp"),
            P("group"),
            P("group"),
            P("group"),
        ),
        out_specs=(
            P(("group", "dp"), "mp"),
            P(("group", "dp"), "mp", None),
            P(("group", "dp"), None, "mp"),
        ),
        check_vma=False,
    )
```

profile of v0, /device:TPU:0, one launch (start us, length us, event | category | flops | bytes accessed | tf_op | source)
XLA Modules:
  0.0 331.1 jit_solution(2888750691558173663)
XLA Ops:
  8.7 2.0 fusion.75
  10.7 10.7 %compare_select_fusion.2 = s32[96]{0:T(128)S(1)} fusion(s32[96]{0:T(128)} %param.14, s32[]{:T(128)} %bitcast.5, s32[]{:T(128)} %bitcast.6, s32[]{:T(128)} %bitcast.7, s32[]{:T(128)} %bitcast.8, s32[]{:T(128)} %bitcast.9, s32[]{:T(128)} %bitcast.10, s32[]{:T(128)} %bitcast.11, s32[]{:T(128)} %bitcast.12, s32[]{:T(128)} %bitcast.13, s32[]{:T(128)} %bitcast.14, ...), kind=kLoop, calls=%fused_computation.89 | loop fusion | flops 3168 | bytes 832 | tf_op jit(solution)/shard_map/gather | solution.py:35
  22.9 2.5 fusion.13
  25.5 2.0 copy.76
  27.5 7.4 %all-to-all-start.1 = ((bf16[8,2,128,512]{3,2,1,0:T(8,128)(2,1)}), bf16[8,2,128,512]{3,2,1,0:T(8,128)(2,1)S(1)}, u32[]{:S(2)}, u32[]{:S(2)}) async-start(bf16[8,2,128,512]{3,2,1,0:T(8,128)(2,1)} %copy.76), calls=%async_computation.2 | async-start | bytes 4194304 | tf_op jit(solution)/shard_map/all_to_all | solution.py:86
  35.8 103.0 %all_gather.11 = bf16[16,32,512]{2,1,0:T(8,128)(2,1)S(1)} all-gather(bf16[2,32,512]{2,1,0:T(8,128)(2,1)S(1)} %copy-done.1), channel_id=1, replica_groups=mesh['group'=2,'dp'=8,'mp'=2] {'dp'}, dimensions={0}, use_global_device_ids=true | all-gather | bytes 589824 | tf_op jit(solution)/shard_map/all_gather | solution.py:76
  141.0 2.8 fusion.24
  143.9 11.7 %fusion.76 = f32[1536,1024]{1,0:T(8,128)} fusion(bf16[1536,2048]{1,0:T(8,128)(2,1)} %param.8, bf16[2048,1024]{1,0:T(8,128)(2,1)} %all-gather.3.cloned.1.call-done), kind=kOutput, calls=%fused_computation.130 | convolution fusion | flops 6442450944 | bytes 16777216 | tf_op jit(solution)/shard_map/dot_general | solution.py:88
  155.7 24.7 %all-gather.5.cloned.1.call-done = bf16[16,2048,32]{1,2,0:T(8,128)(2,1)} async-done(((bf16[2,2048,32]{1,2,0:T(8,128)(2,1)}), bf16[16,2048,32]{1,2,0:T(8,128)(2,1)}) %all-gather.5.cloned.1.call-update) | async-done | bytes 2097168 | tf_op jit(solution)/shard_map/all_gather | solution.py:75
  180.4 4.0 %convolution_convert_fusion.1 = bf16[12,2048,32]{1,0,2:T(8,128)(2,1)S(1)} fusion(bf16[16,2048,32]{1,2,0:T(8,128)(2,1)} %all-gather.5.cloned.1.call-done, s32[12]{0:T(128)S(1)} %fusion.60), kind=kOutput, calls=%fused_computation.4 | convolution fusion | flops 25952448 | bytes 3670064 | tf_op jit(solution)/shard_map/jp,pdq->jdq/dot_general | solution.py:80
  184.5 5.1 %fusion.21 = f32[12,128,32]{1,2,0:T(8,128)S(1)} fusion(bf16[12,128,2048]{2,1,0:T(8,128)(2,1)} %bitcast.95, bf16[12,2048,32]{1,0,2:T(8,128)(2,1)S(1)} %convolution_convert_fusion.1), kind=kOutput, calls=%fused_computation.27 | convolution fusion | flops 201326592 | bytes 8060928 | tf_op jit(solution)/shard_map/tbd,tdq->tbq/dot_general | solution.py:93
  189.6 4.1 %all-reduce.4 = bf16[12,128,32]{1,2,0:T(8,128)(2,1)S(1)} all-reduce(f32[12,128,32]{1,2,0:T(8,128)S(1)} %fusion.21), channel_id=1, replica_groups=mesh['group'=2,'dp'=8,'mp'=2] {'mp'}, use_global_device_ids=true, to_apply=%region_3.4 | all-reduce | flops 49152 | bytes 294912 | tf_op jit(solution)/shard_map/psum | solution.py:95
  195.7 3.5 %all-to-all-start.3 = ((bf16[8,2,32,512]{3,1,2,0:T(2,128)(2,1)}), bf16[8,2,32,512]{3,1,2,0:T(2,128)(2,1)S(1)}, u32[]{:S(2)}, u32[]{:S(2)}) async-start(bf16[8,2,32,512]{3,1,2,0:T(2,128)(2,1)} %copy.81), calls=%async_computation.4 | async-start | bytes 1048576 | tf_op jit(solution)/shard_map/all_to_all | solution.py:145
  199.3 3.9 %fusion = bf16[12,2048,32,1]{1,2,0,3:T(8,128)(2,1)S(1)} fusion(bf16[12,128,2048]{2,1,0:T(8,128)(2,1)} %bitcast.96, f32[12,128,32]{1,2,0:T(8,128)} %all-reduce.3.cloned.1.call-done), kind=kOutput, calls=%fused_computation.6 | convolution fusion | flops 202211328 | bytes 8060928 | tf_op jit(solution)/shard_map/tbd,tbq->tdq/dot_general | solution.py:124
  204.4 3.5 %copy.78 = bf16[8,2,2048,32]{2,1,3,0:T(2,128)(2,1)} copy(bf16[8,2,2048,32]{2,0,1,3:T(8,128)(2,1)S(1)} %convolution_convert_fusion) | data formatting | bytes 4194304 | tf_op jit(solution)/shard_map/convert_element_type | solution.py:139
  207.8 6.6 %all-to-all-done.3 = bf16[8,2,32,512]{3,1,2,0:T(2,128)(2,1)S(1)} async-done(((bf16[8,2,32,512]{3,1,2,0:T(2,128)(2,1)}), bf16[8,2,32,512]{3,1,2,0:T(2,128)(2,1)S(1)}, u32[]{:S(2)}, u32[]{:S(2)}) %all-to-all-start.3) | async-done | bytes 524320 | tf_op jit(solution)/shard_map/all_to_all | solution.py:145
  214.5 3.6 %all-to-all-start.2 = ((bf16[8,2,2048,32]{2,1,3,0:T(2,128)(2,1)}), bf16[8,2,2048,32]{2,1,3,0:T(2,128)(2,1)S(1)}, u32[]{:S(2)}, u32[]{:S(2)}) async-start(bf16[8,2,2048,32]{2,1,3,0:T(2,128)(2,1)} %copy.78), calls=%async_computation.3 | async-start | bytes 4194304 | tf_op jit(solution)/shard_map/all_to_all | solution.py:144
  218.1 2.6 fusion.18
  221.9 3.0 copy.71
  224.8 41.7 %all-to-all-done.2 = bf16[8,2,2048,32]{2,1,3,0:T(2,128)(2,1)S(1)} async-done(((bf16[8,2,2048,32]{2,1,3,0:T(2,128)(2,1)}), bf16[8,2,2048,32]{2,1,3,0:T(2,128)(2,1)S(1)}, u32[]{:S(2)}, u32[]{:S(2)}) %all-to-all-start.2) | async-done | bytes 2097184 | tf_op jit(solution)/shard_map/all_to_all | solution.py:144
  266.5 4.6 %all-to-all-start = ((bf16[8,2,128,512]{3,1,2,0:T(2,128)(2,1)}), bf16[8,2,128,512]{3,1,2,0:T(2,128)(2,1)}, u32[]{:S(2)}, u32[]{:S(2)}) async-start(bf16[8,2,128,512]{3,1,2,0:T(2,128)(2,1)} %copy.71), calls=%async_computation.1 | async-start | bytes 4194304 | tf_op jit(solution)/shard_map/all_to_all | solution.py:110
  274.8 44.0 %all-to-all-done = bf16[8,2,128,512]{3,1,2,0:T(2,128)(2,1)} async-done(((bf16[8,2,128,512]{3,1,2,0:T(2,128)(2,1)}), bf16[8,2,128,512]{3,1,2,0:T(2,128)(2,1)}, u32[]{:S(2)}, u32[]{:S(2)}) %all-to-all-start) | async-done | bytes 2097184 | tf_op jit(solution)/shard_map/all_to_all | solution.py:110
  318.8 2.9 bitcast_convert_fusion
  321.7 2.0 copy.73
  (56 shorter events, 13.4 us)
Async XLA Ops:
  8.0 135.9 %all-gather.3.cloned.1.call-start = ((), (), s32[]{:S(2)}) async-start(), calls=%async_computation.5 | async-start | bytes 4718592 | tf_op jit(solution)/shard_map/all_gather | solution.py:90
  27.5 8.2 %copy-start.1 = (bf16[2,32,512]{2,1,0:T(8,128)(2,1)S(1)}, bf16[2,32,512]{2,1,0:T(8,128)(2,1)}, u32[]{:S(2)}) copy-start(bf16[2,32,512]{2,1,0:T(8,128)(2,1)} %param.11) | copy-start | bytes 196612
  27.5 111.7 %all-to-all-start.1 = ((bf16[8,2,128,512]{3,2,1,0:T(8,128)(2,1)}), bf16[8,2,128,512]{3,2,1,0:T(8,128)(2,1)S(1)}, u32[]{:S(2)}, u32[]{:S(2)}) async-start(bf16[8,2,128,512]{3,2,1,0:T(8,128)(2,1)} %copy.76), calls=%async_computation.2 | async-start | bytes 4194304 | tf_op jit(solution)/shard_map/all_to_all | solution.py:86
  34.9 145.6 %all-gather.5.cloned.1.call-start = ((), (), s32[]{:S(2)}) async-start(), calls=%async_computation.7 | async-start | bytes 2359296 | tf_op jit(solution)/shard_map/all_gather | solution.py:75
  35.6 163.6 %all-reduce.3.cloned.1.call-start = ((), (), s32[]{:S(2)}) async-start(), calls=%async_computation.8 | async-start | bytes 393216 | tf_op jit(solution)/shard_map/psum | solution.py:122
  143.8 74.3 %reduce-scatter.2.cloned.1.call-start = ((), (), s32[]{:S(2)}) async-start(), calls=%async_computation.6 | async-start | bytes 9437184 | tf_op jit(solution)/shard_map/reduce_scatter | solution.py:94
  184.5 9.3 %copy-start = (bf16[12,128,512]{2,1,0:T(8,128)(2,1)S(1)}, bf16[12,128,512]{2,1,0:T(8,128)(2,1)}, u32[]{:S(2)}) copy-start(bf16[12,128,512]{2,1,0:T(8,128)(2,1)} %gather_fusion) | copy-start | bytes 4718596
  195.7 18.7 %all-to-all-start.3 = ((bf16[8,2,32,512]{3,1,2,0:T(2,128)(2,1)}), bf16[8,2,32,512]{3,1,2,0:T(2,128)(2,1)S(1)}, u32[]{:S(2)}, u32[]{:S(2)}) async-start(bf16[8,2,32,512]{3,1,2,0:T(2,128)(2,1)} %copy.81), calls=%async_computation.4 | async-start | bytes 1048576 | tf_op jit(solution)/shard_map/all_to_all | solution.py:145
  214.5 52.1 %all-to-all-start.2 = ((bf16[8,2,2048,32]{2,1,3,0:T(2,128)(2,1)}), bf16[8,2,2048,32]{2,1,3,0:T(2,128)(2,1)S(1)}, u32[]{:S(2)}, u32[]{:S(2)}) async-start(bf16[8,2,2048,32]{2,1,3,0:T(2,128)(2,1)} %copy.78), calls=%async_computation.3 | async-start | bytes 4194304 | tf_op jit(solution)/shard_map/all_to_all | solution.py:144
  266.5 52.2 %all-to-all-start = ((bf16[8,2,128,512]{3,1,2,0:T(2,128)(2,1)}), bf16[8,2,128,512]{3,1,2,0:T(2,128)(2,1)}, u32[]{:S(2)}, u32[]{:S(2)}) async-start(bf16[8,2,128,512]{3,1,2,0:T(2,128)(2,1)} %copy.71), calls=%async_computation.1 | async-start | bytes 4194304 | tf_op jit(solution)/shard_map/all_to_all | solution.py:110
Sparse Core Ops, SparseCore 0:
  10.9 116.1 all-gather.2
  129.4 51.0 all-gather.4
Sparse Core Ops, SparseCore 1:
  143.9 19.1 all-reduce.2
  165.3 15.5 reduce-scatter.1
where the time goes:
time: 332 us; the launch traced here: 331 us
  waiting for transfers between devices  118 us (36%)
  blocking collectives  107 us (32%)
  matrix products  40.8 us (12%)
  starting transfers between devices  19.2 us (6%)
  local copies, waits for them, and re-layouts  18.5 us (6%)
  between operations  15.8 us (5%)
  other arithmetic  11.3 us (3%)
    all_gather x1, blocking collectives, on_device(): lax.all_gather(adapter_up_weight, 'dp', axis=0, tiled=True)  103 us
    all_to_all x1, waiting for transfers between devices, on_device(): lax.all_to_all(send_rows, 'dp', split_axis=0, concat_axis=0, tiled=True)  44 us
    all_to_all x1, waiting for transfers between devices, on_device(): lax.all_to_all(send_down_term, 'dp', split_axis=0, concat_axis=0, tiled=T...  41.7 us
    all_gather x1, waiting for transfers between devices, on_device(): lax.all_gather(adapter_down_weight, 'dp', axis=0, tiled=True)  24.7 us
    dot_general x1, matrix products, on_device(): jnp.dot(input_tiles, lax.all_gather(value_matrix, 'dp', axis=1, tiled=Tru...  11.7 us
    gather x1, other arithmetic, on_device(): tenant_storage_row[tile_owner_tenant].reshape(ranks, per_rank)  10.7 us
    all_to_all x1, starting transfers between devices, on_device(): lax.all_to_all(send_grad, 'dp', split_axis=0, concat_axis=0, tiled=True)  7.38 us
  transfers between devices with their start and end apart: 8, of which 4 were waited for; matrix products, arithmetic and copies ran while one was open for 20% of the time, Pallas kernels for 0%

commit v1 on v0

v1 whole, which is shorter than its diff:
```python
import jax
import jax.numpy as jnp
from jax import lax
from jax.sharding import PartitionSpec as P

ROWS = 128
SCALE = 0.25
F32 = jnp.float32
BF16 = jnp.bfloat16


def levels_of(labels, count):
    per_rank = labels.shape[1]
    positions = jnp.arange(per_rank, dtype=jnp.int32)
    earlier = positions[:, None] < positions[None, :]
    same = labels[:, :, None] == labels[:, None, :]
    found = jnp.sum((same & earlier[None]).astype(jnp.int32), axis=1)
    return jnp.minimum(found, count - 1)


def on_device(x, w, a, b, dy, target, tenant, storage):
    ranks = lax.axis_size("dp")
    me = lax.axis_index("dp")
    half = lax.axis_index("mp")
    tiles = x.shape[0] // ROWS
    slots = dy.shape[0] // ROWS
    owned, depth, rank = a.shape
    cols = dy.shape[1]
    places = owned * ranks
    level_count = (tiles + ranks - 1) // ranks

    packed = jnp.concatenate([a.transpose(0, 2, 1), b], axis=2).reshape(owned * rank, depth + cols)
    packed = lax.all_gather(packed, "dp", axis=0, tiled=True)
    w_all = lax.all_gather(w, "dp", axis=0)
    a_all = packed[:, :depth].reshape(places, rank, depth)
    b_all = packed[:, depth:]

    place = storage[tenant].reshape(ranks, tiles)
    goal = target.reshape(ranks, tiles)
    dest = jnp.where(goal >= 0, goal // slots, -1)
    level = levels_of(dest, level_count)
    my_place, my_dest, my_level = place[me], dest[me], level[me]
    slot_ids = me * slots + jnp.arange(slots, dtype=jnp.int32)
    hit = goal.reshape(-1)[None, :] == slot_ids[:, None]
    filled = jnp.any(hit, axis=1)
    source = jnp.argmax(hit, axis=1).astype(jnp.int32)
    slot_src, slot_level = source // tiles, level.reshape(-1)[source]
    slot_place = place.reshape(-1)[source]
    lanes = jnp.arange(ranks * level_count, dtype=jnp.int32)
    tile_lane = jnp.where(my_dest >= 0, my_dest * level_count + my_level, -1)
    slot_lane = jnp.where(filled, slot_src * level_count + slot_level, -1)
    lane_tile = jnp.argmax(tile_lane[None, :] == lanes[:, None], axis=1)
    lane_slot = jnp.argmax(slot_lane[None, :] == lanes[:, None], axis=1)

    xt = x.reshape(tiles, ROWS, depth)
    dyt = dy.reshape(slots, ROWS, cols)
    low_part = jnp.einsum("tqd,tbd->tqb", a_all[my_place], xt, preferred_element_type=F32)
    grad_part = jnp.einsum(
        "sqk,sbk->sqb",
        b_all.reshape(places, rank, cols)[slot_place],
        dyt,
        preferred_element_type=F32,
    )
    both = lax.psum(jnp.concatenate([low_part, grad_part], axis=0), "mp")
    low = both[:tiles].astype(BF16)
    low_grad = (SCALE * both[tiles:]).astype(BF16)
    sent = jnp.concatenate(
        [
            low[lane_tile].reshape(ranks, level_count, rank, ROWS),
            low_grad[lane_slot].reshape(ranks, level_count, rank, ROWS),
        ],
        axis=1,
    )
    got = lax.all_to_all(sent, "dp", split_axis=0, concat_axis=0, tiled=True)
    slot_low = got[:, :level_count].reshape(-1, rank, ROWS)[jnp.maximum(slot_lane, 0)]
    tile_grad = got[:, level_count:].reshape(-1, rank, ROWS)[jnp.maximum(tile_lane, 0)]

    def spread(values, where, keep):
        on = (where[None, :] == jnp.arange(places, dtype=jnp.int32)[:, None]) & keep[None, :]
        full = jnp.where(
            on[:, None, :, None], values.transpose(1, 0, 2)[None], jnp.zeros((), values.dtype)
        )
        return full.reshape(places * rank, -1)

    here = my_dest >= 0
    a_sum = jnp.dot(spread(tile_grad, my_place, here), x, preferred_element_type=F32)
    b_sum = SCALE * jnp.dot(spread(slot_low, slot_place, filled), dy, preferred_element_type=F32)
    sums = jnp.concatenate([a_sum.astype(BF16), b_sum.astype(BF16)], axis=1)
    sums = lax.psum_scatter(sums, "dp", scatter_dimension=0, tiled=True).astype(F32)
    grad_a = sums[:, :depth].reshape(owned, rank, depth).transpose(0, 2, 1)
    grad_b = sums[:, depth:].reshape(owned, rank, cols)

    def project(which):
        part = lax.dynamic_slice_in_dim(w_all, which * (ranks // 2), ranks // 2, 0)
        part = part.transpose(1, 0, 2).reshape(depth, cols)
        return jnp.dot(x, part, preferred_element_type=F32)

    other = lax.ppermute(project(1 - half).astype(BF16), "mp", [(0, 1), (1, 0)])
    low_wide = spread(low, my_place, jnp.ones((tiles,), bool))
    adapted = lax.dot_general(
        low_wide, b_all, (((0,), (0,)), ((), ())), preferred_element_type=F32
    )
    y = (project(half) + SCALE * adapted + other.astype(F32)).astype(BF16)
    y = y.reshape(tiles, ROWS, cols)[lane_tile].reshape(ranks, level_count, ROWS, cols)
    y = lax.all_to_all(y, "dp", split_axis=0, concat_axis=0, tiled=True)
    moved = y.reshape(-1, ROWS, cols)[jnp.maximum(slot_lane, 0)]
    moved = jnp.where(filled[:, None, None], moved, jnp.zeros((), BF16))
    return moved.reshape(slots * ROWS, cols), grad_a, grad_b


def solution(mesh):
    return jax.shard_map(
        on_device,
        mesh=mesh,
        in_specs=(
            P(("group", "dp"), "mp"),
            P("mp", "dp"),
            P(("group", "dp"), "mp", None),
            P(("group", "dp"), None, "mp"),
            P(("group", "dp"), "mp"),
            P("group"),
            P("group"),
            P("group"),
        ),
        out_specs=(
            P(("group", "dp"), "mp"),
            P(("group", "dp"), "mp", None),
            P(("group", "dp"), None, "mp"),
        ),
        check_vma=False,
    )
```

time: 332 us -> 311 us (0.937)
  blocking collectives: 107 us -> 0 us
  waiting for transfers between devices: 118 us -> 194 us
  local copies, waits for them, and re-layouts: 18.5 us -> 38 us
  other arithmetic: 11.3 us -> 23.2 us
  matrix products: 40.8 us -> 30.1 us
  starting transfers between devices: 19.2 us -> 10.5 us
    all_gather x1 -> x0, blocking collectives: 103 us -> none  [on_device(): lax.all_gather(adapter_up_weight, 'dp', axis=0, tiled=True)]
    all_to_all x4 -> x2, waiting for transfers between devices: 92.3 us -> 12.6 us  [the longest x1 12.6 us: on_device(): got = lax.all_to_all(sent, 'dp', split_axis=0, concat_axis=0, tiled=True)]
    reduce_scatter x1, waiting for transfers between devices: 0.03 us -> 75.2 us  [on_device(): lax.psum_scatter(sums, 'dp', scatter_dimension=0, tiled=True).astype(F32)]
    all_gather x2, waiting for transfers between devices: 24.8 us -> 91.9 us  [the longest x1 47.7 us: on_device(): w_all = lax.all_gather(w, 'dp', axis=0)]
    psum x1, waiting for transfers between devices: 0.03 us -> 13.7 us  [on_device(): both = lax.psum(jnp.concatenate([low_part, grad_part], axis=0), 'mp')]
    transpose x0 -> x7, local copies, waits for them, and re-layouts: none -> 13.6 us  [the longest x3 12.5 us: project(): part = part.transpose(1, 0, 2).reshape(depth, cols)]
    dot_general x15 -> x7, matrix products: 40.8 us -> 30.1 us  [the longest x2 14.6 us: project(): return jnp.dot(x, part, preferred_element_type=F32)]
    convert_element_type x5 -> x1, local copies, waits for them, and re-layouts: 11.7 us -> 1.73 us  [on_device(): y = (project(half) + SCALE * adapted + other.astype(F32)).astype(BF16)]
  transfers between devices with their start and end apart: 8 -> 7, of which waited for: 4 -> 5; matrix products, arithmetic and copies ran while one was open for 20% -> 18% of each run, Pallas kernels for 0% -> 0%
where the time goes in v1:
time: 311 us; the launch traced here: 310 us
  waiting for transfers between devices  194 us (62%)
  local copies, waits for them, and re-layouts  38 us (12%)
  matrix products  30.1 us (10%)
  other arithmetic  23.2 us (7%)
  between operations  14.1 us (5%)
  starting transfers between devices  10.5 us (3%)
    reduce_scatter x1, waiting for transfers between devices, on_device(): lax.psum_scatter(sums, 'dp', scatter_dimension=0, tiled=True).astype(F32)  75.2 us
    all_gather x1, waiting for transfers between devices, on_device(): w_all = lax.all_gather(w, 'dp', axis=0)  47.7 us
    all_gather x1, waiting for transfers between devices, on_device(): packed = lax.all_gather(packed, 'dp', axis=0, tiled=True)  44.2 us
    dot_general x2, matrix products, project(): return jnp.dot(x, part, preferred_element_type=F32)  14.6 us
    psum x1, waiting for transfers between devices, on_device(): both = lax.psum(jnp.concatenate([low_part, grad_part], axis=0), 'mp')  13.7 us
    all_to_all x1, waiting for transfers between devices, on_device(): got = lax.all_to_all(sent, 'dp', split_axis=0, concat_axis=0, tiled=True)  12.6 us
    transpose x3, local copies, waits for them, and re-layouts, project(): part = part.transpose(1, 0, 2).reshape(depth, cols)  12.5 us
    gather x1, other arithmetic, on_device(): place = storage[tenant].reshape(ranks, tiles)  10.7 us
  transfers between devices with their start and end apart: 7, of which 5 were waited for; matrix products, arithmetic and copies ran while one was open for 18% of the time, Pallas kernels for 0%

profile of v1, /device:TPU:0, one launch (start us, length us, event | category | flops | bytes accessed | tf_op | source)
XLA Modules:
  0.0 310.0 jit_solution(10050571017169007362)
XLA Ops:
  7.2 1.8 pad_maximum_fusion.2
  9.1 1.9 fusion.26
  11.1 10.7 %compare_select_fusion.6 = s32[96]{0:T(128)S(1)} fusion(s32[96]{0:T(128)} %param.14, s32[]{:T(128)} %bitcast.5, s32[]{:T(128)} %bitcast.6, s32[]{:T(128)} %bitcast.7, s32[]{:T(128)} %bitcast.8, s32[]{:T(128)} %bitcast.9, s32[]{:T(128)} %bitcast.10, s32[]{:T(128)} %bitcast.11, s32[]{:T(128)} %bitcast.12, s32[]{:T(128)} %bitcast.13, s32[]{:T(128)} %bitcast.14, ...), kind=kLoop, calls=%fused_computation.68 | loop fusion | flops 3168 | bytes 832 | tf_op jit(solution)/shard_map/gather | solution.py:38
  23.9 44.2 %all-gather.4.cloned.1.call-done = bf16[512,2560]{1,0:T(8,128)(2,1)} async-done(((bf16[64,2560]{1,0:T(8,128)(2,1)}), bf16[512,2560]{1,0:T(8,128)(2,1)}) %all-gather.4.cloned.1.call-update) | async-done | bytes 2621456 | tf_op jit(solution)/shard_map/all_gather | solution.py:33
  70.4 3.2 %slice.70 = bf16[512,2048]{1,0:T(8,128)(2,1)} slice(bf16[512,2560]{1,0:T(8,128)(2,1)} %all-gather.4.cloned.1.call-done), slice={[0:512], [0:2048]} | slice | bytes 4194304 | tf_op jit(solution)/shard_map/slice | solution.py:35
  73.6 2.2 gather_fusion
  75.9 5.0 %fusion.27 = f32[12,32,128]{2,1,0:T(8,128)S(1)} fusion(bf16[12,32,2048]{2,1,0:T(8,128)(2,1)S(1)} %gather_fusion, bf16[12,128,2048]{2,1,0:T(8,128)(2,1)} %bitcast.103), kind=kOutput, calls=%fused_computation.104 | convolution fusion | flops 201326592 | bytes 8060928 | tf_op jit(solution)/shard_map/tqd,tbd->tqb/dot_general | solution.py:57
  85.3 13.7 %all-reduce.2.cloned.1.call-done = f32[24,32,128]{2,1,0:T(8,128)} async-done(((f32[24,32,128]{2,1,0:T(8,128)}), f32[24,32,128]{2,1,0:T(8,128)}) %all-reduce.2.cloned.1.call-update) | async-done | bytes 393232 | tf_op jit(solution)/shard_map/psum | solution.py:64
  102.7 5.8 %all-to-all-start.1 = ((bf16[8,4,32,128]{3,2,1,0:T(8,128)(2,1)}), bf16[8,4,32,128]{3,2,1,0:T(8,128)(2,1)S(1)}, u32[]{:S(2)}, u32[]{:S(2)}) async-start(bf16[8,4,32,128]{3,2,1,0:T(8,128)(2,1)} %pad_maximum_fusion.3), calls=%async_computation.1 | async-start | bytes 524288 | tf_op jit(solution)/shard_map/all_to_all | solution.py:74
  109.8 12.6 %all-to-all-done.1 = bf16[8,4,32,128]{3,2,1,0:T(8,128)(2,1)S(1)} async-done(((bf16[8,4,32,128]{3,2,1,0:T(8,128)(2,1)}), bf16[8,4,32,128]{3,2,1,0:T(8,128)(2,1)S(1)}, u32[]{:S(2)}, u32[]{:S(2)}) %all-to-all-start.1) | async-done | bytes 262176 | tf_op jit(solution)/shard_map/all_to_all | solution.py:74
  124.1 1.8 fusion.14
  126.8 4.7 %convolution_convert_fusion = bf16[512,2048]{1,0:T(8,128)(2,1)} fusion(bf16[1536,2048]{1,0:T(8,128)(2,1)S(1)} %bitcast.105, bf16[64,8,12,128]{3,2,1,0:T(8,128)(2,1)S(1)} %bitcast.108), kind=kOutput, calls=%fused_computation.14 | convolution fusion | flops 3222274048 | bytes 9961472 | tf_op jit(solution)/shard_map/dot_general | solution.py:86
  131.5 47.7 %all-gather.6.cloned.1.call-done = bf16[16384,128]{1,0:T(8,128)(2,1)} async-done(((bf16[2048,128]{1,0:T(8,128)(2,1)}), bf16[16384,128]{1,0:T(8,128)(2,1)}) %all-gather.6.cloned.1.call-update) | async-done | bytes 4194320 | tf_op jit(solution)/shard_map/all_gather | solution.py:34
  179.2 4.5 %dynamic-slice_bitcast_fusion.1 = (bf16[2048,4,128]{2,0,1:T(8,128)(2,1)}, bf16[2048,4,128]{2,0,1:T(8,128)(2,1)}) fusion(bf16[8,2048,128]{2,1,0:T(8,128)(2,1)} %bitcast.106, s32[]{:T(128)S(6)} %select_n.131, s32[]{:T(128)S(6)} %select_n.139), kind=kLoop, calls=%fused_computation.19 | loop fusion | bytes 8388616 | tf_op jit(solution)/shard_map/transpose | solution.py:95
  183.7 4.0 %copy.31 = bf16[2048,4,128]{0,2,1:T(8,128)(2,1)} copy(bf16[2048,4,128]{2,0,1:T(8,128)(2,1)} %get-tuple-element.14) | data formatting | bytes 4194304 | tf_op jit(solution)/shard_map/transpose | solution.py:95
  187.7 8.2 %fusion.1 = bf16[1536,512]{0,1:T(8,128)(2,1)} fusion(bf16[2048,512]{0,1:T(8,128)(2,1)} %bitcast.109, bf16[1536,2048]{1,0:T(8,128)(2,1)} %param.8), kind=kOutput, calls=%fused_computation.16 | convolution fusion | flops 3222011904 | bytes 9961472 | tf_op jit(solution)/shard_map/dot_general | solution.py:96
  199.2 4.0 %copy.28 = bf16[2048,4,128]{0,2,1:T(8,128)(2,1)} copy(bf16[2048,4,128]{2,0,1:T(8,128)(2,1)} %get-tuple-element.13) | data formatting | bytes 4194304 | tf_op jit(solution)/shard_map/transpose | solution.py:95
  203.2 6.4 %convolution_bitcast_fusion = f32[1536,512]{0,1:T(8,128)S(1)} fusion(bf16[2048,512]{0,1:T(8,128)(2,1)} %bitcast.110, bf16[1536,2048]{1,0:T(8,128)(2,1)} %param.8), kind=kOutput, calls=%fused_computation.12 | convolution fusion | flops 3221225472 | bytes 11534336 | tf_op jit(solution)/shard_map/dot_general | solution.py:96
  209.6 3.5 %add_convert_fusion = bf16[1536,512]{0,1:T(8,128)(2,1)} fusion(bf16[1536,512]{0,1:T(8,128)(2,1)S(1)} %collective-permute-done, f32[1536,512]{0,1:T(8,128)S(1)} %convolution_bitcast_fusion, bf16[64,8,12,128]{3,2,1,0:T(8,128)(2,1)S(1)} %bitcast.101, bf16[512,2560]{1,0:T(8,128)(2,1)} %all-gather.4.cloned.1.call-done), kind=kOutput, calls=%fused_computation.13 | convolution fusion | flops 809238528 | bytes 8388608 | tf_op jit(solution)/shard_map/dot_general | solution.py:100
  214.8 2.1 gather_fusion.3
  216.9 4.4 %all-to-all-start = ((bf16[8,2,128,512]{3,2,1,0:T(8,128)(2,1)}), bf16[8,2,128,512]{3,2,1,0:T(8,128)(2,1)}, u32[]{:S(2)}, u32[]{:S(2)}) async-start(bf16[8,2,128,512]{3,2,1,0:T(8,128)(2,1)} %bitcast.100), calls=%async_computation | async-start | bytes 4194304 | tf_op jit(solution)/shard_map/all_to_all | solution.py:105
  221.3 75.2 %reduce-scatter.2.cloned.1.call-done = bf16[64,2560]{1,0:T(8,128)(2,1)} async-done(((bf16[512,2560]{1,0:T(8,128)(2,1)}), bf16[64,2560]{1,0:T(8,128)(2,1)}) %reduce-scatter.2.cloned.1.call-update) | async-done | bytes 327696 | tf_op jit(solution)/shard_map/reduce_scatter | solution.py:89
  296.5 1.8 slice.76
  299.8 2.2 gather_fusion.5
  (86 shorter events, 24.4 us)
Async XLA Ops:
  7.2 62.7 %copy-start = (bf16[1536,512]{1,0:T(8,128)(2,1)S(1)}, bf16[1536,512]{1,0:T(8,128)(2,1)}, u32[]{:S(2)}) copy-start(bf16[1536,512]{1,0:T(8,128)(2,1)} %param.12) | copy-start | bytes 4718596
  7.2 61.0 %all-gather.4.cloned.1.call-start = ((), (), s32[]{:S(2)}) async-start(), calls=%async_computation.3 | async-start | bytes 2949120 | tf_op jit(solution)/shard_map/all_gather | solution.py:33
  9.1 89.8 %all-reduce.2.cloned.1.call-start = ((), (), s32[]{:S(2)}) async-start(), calls=%async_computation.4 | async-start | bytes 786432 | tf_op jit(solution)/shard_map/psum | solution.py:64
  75.9 6.6 %copy-start.4 = (s32[96]{0:T(128)S(1)}, s32[96]{0:T(128)}, u32[]{:S(2)}) copy-start(s32[96]{0:T(128)} %param.13) | copy-start | bytes 1156
  81.7 97.5 %all-gather.6.cloned.1.call-start = ((), (), s32[]{:S(2)}) async-start(), calls=%async_computation.6 | async-start | bytes 4718592 | tf_op jit(solution)/shard_map/all_gather | solution.py:34
  102.7 19.6 %all-to-all-start.1 = ((bf16[8,4,32,128]{3,2,1,0:T(8,128)(2,1)}), bf16[8,4,32,128]{3,2,1,0:T(8,128)(2,1)S(1)}, u32[]{:S(2)}, u32[]{:S(2)}) async-start(bf16[8,4,32,128]{3,2,1,0:T(8,128)(2,1)} %pad_maximum_fusion.3), calls=%async_computation.1 | async-start | bytes 524288 | tf_op jit(solution)/shard_map/all_to_all | solution.py:74
  108.5 188.0 %reduce-scatter.2.cloned.1.call-start = ((), (), s32[]{:S(2)}) async-start(), calls=%async_computation.5 | async-start | bytes 2949120 | tf_op jit(solution)/shard_map/reduce_scatter | solution.py:89
  123.6 2.2 slice-start
  124.1 2.8 slice-start.1
  187.7 8.2 %copy-start.2 = (bf16[512,2048]{1,0:T(8,128)(2,1)S(1)}, bf16[512,2048]{1,0:T(8,128)(2,1)}, u32[]{:S(2)}) copy-start(bf16[512,2048]{1,0:T(8,128)(2,1)} %convolution_convert_fusion) | copy-start | bytes 6291460
  187.7 8.2 %copy-start.3 = (bf16[512,512]{1,0:T(8,128)(2,1)S(1)}, bf16[512,512]{1,0:T(8,128)(2,1)}, u32[]{:S(2)}) copy-start(bf16[512,512]{1,0:T(8,128)(2,1)} %fusion.14) | copy-start | bytes 1572868
  195.9 13.7 %collective-permute-start = (bf16[1536,512]{0,1:T(8,128)(2,1)}, bf16[1536,512]{0,1:T(8,128)(2,1)S(1)}, u32[]{:S(2)}, u32[]{:S(2)}) collective-permute-start(bf16[1536,512]{0,1:T(8,128)(2,1)} %fusion.1), channel_id=1, source_target_pairs={{0,1},{1,0},{2,3},{3,2},{4,5},{5,4},{6,7},{7,6},{8,9},{9,8},{10,11... | collective-permute-start | bytes 4718600 | tf_op jit(solution)/shard_map/ppermute | solution.py:98
  203.2 6.4 %copy-start.1 = (bf16[16,32,12,128]{3,2,1,0:T(8,128)(2,1)S(1)}, bf16[16,32,12,128]{3,2,1,0:T(8,128)(2,1)}, u32[]{:S(2)}) copy-start(bf16[16,32,12,128]{3,2,1,0:T(8,128)(2,1)} %broadcast_select_fusion.2) | copy-start | bytes 4718596
  216.9 82.9 %all-to-all-start = ((bf16[8,2,128,512]{3,2,1,0:T(8,128)(2,1)}), bf16[8,2,128,512]{3,2,1,0:T(8,128)(2,1)}, u32[]{:S(2)}, u32[]{:S(2)}) async-start(bf16[8,2,128,512]{3,2,1,0:T(8,128)(2,1)} %bitcast.100), calls=%async_computation | async-start | bytes 4194304 | tf_op jit(solution)/shard_map/all_to_all | solution.py:105
Sparse Core Ops, SparseCore 0:
  10.8 57.3 all-gather.3
  81.8 17.0 all-reduce.1
  101.3 77.8 all-gather.5
  197.7 98.6 reduce-scatter.1

commit v2 on v1

--- a/solution.py
+++ b/solution.py
@@ -1,6 +1,8 @@
 import jax
 import jax.numpy as jnp
 from jax import lax
+from jax.experimental import pallas as pl
+from jax.experimental.pallas import tpu as pltpu
 from jax.sharding import PartitionSpec as P
 
 ROWS = 128
@@ -107,10 +109,346 @@
     moved = jnp.where(filled[:, None, None], moved, jnp.zeros((), BF16))
     return moved.reshape(slots * ROWS, cols), grad_a, grad_b
 
+MESH = pl.DeviceIdType.MESH
+NT = (((1,), (1,)), ((), ()))
+
+
+def rank_at(pos):
+    pos = lax.rem(pos + 16, 8)
+    return jnp.where(pos < 4, 2 * pos, 15 - 2 * pos)
+
+
+def kernel(
+    tab, x, w, ab, dy,
+    moved, grads,
+    w_all, ab_all, wide, acc, part, part_got, low, grad, swap, swap_got,
+    rs_send, rs_got, half_send, half_got, y, y_send, y_got,
+    own_sem, ab_sem, w_sem, part_sem, swap_sem, rs_sem, half_sem, y_sem,
+):
+    tiles, _, depth = x.shape
+    cols = dy.shape[2]
+    wcols = w.shape[1]
+    me = lax.axis_index("dp")
+    core = lax.axis_index("mp")
+    z, side = me // 2, me % 2
+    pos = jnp.where(side == 0, z, 7 - z)
+    hops = (rank_at(pos + 1), rank_at(pos - 1))
+    o_place, o_got, o_here, o_splace, o_slow, o_sy, o_fill = (tiles * i for i in range(7))
+    o_ltile = 7 * tiles
+    o_lslot = o_ltile + 16
+    zero = jnp.zeros((), BF16)
+
+    def send(source, target, sems, index, device):
+        copy = pltpu.make_async_remote_copy(
+            src_ref=source, dst_ref=target,
+            send_sem=sems.at[(0,) + index], recv_sem=sems.at[(1,) + index],
+            device_id=device, device_id_type=MESH,
+        )
+        copy.start()
+        return copy
+
+    own_ab = pltpu.make_async_copy(ab, ab_all.at[pl.ds(2 * me, 2)], own_sem.at[0])
+    own_w = pltpu.make_async_copy(
+        w, w_all.at[:, pl.ds(pl.multiple_of(me * wcols, wcols), wcols)], own_sem.at[1]
+    )
+    own_ab.start()
+    own_w.start()
+
+    barrier = pltpu.get_barrier_semaphore()
+    for d in range(1, 8):
+        pl.semaphore_signal(
+            barrier, inc=1, device_id={"dp": lax.rem(me + d, 8)}, device_id_type=MESH
+        )
+    pl.semaphore_signal(barrier, inc=1, device_id={"mp": 1 - core}, device_id_type=MESH)
+    pl.semaphore_wait(barrier, 8)
+
+    def ab_step(s):
+        out = []
+        for way in range(2):
+            owner = rank_at(pos - s if way == 0 else pos + s)
+            where = ab_all.at[2 * owner + way]
+            out.append(send(ab.at[way] if s == 0 else where, where, ab_sem, (way, s),
+                            {"dp": hops[way]}))
+        return out
+
+    def w_step(s):
+        out = []
+        rows = depth // 2
+        for way in range(2):
+            owner = rank_at(pos - s if way == 0 else pos + s)
+            there = pl.ds(pl.multiple_of(owner * wcols, wcols), wcols)
+            where = w_all.at[pl.ds(way * rows, rows), there]
+            out.append(send(w.at[pl.ds(way * rows, rows)] if s == 0 else where, where,
+                            w_sem, (way, s), {"dp": hops[way]}))
+        return out
+
+    flying = []
+    for s in range(7):
+        now = ab_step(s)
+        flying += now
+        for copy in now:
+            copy.wait_recv()
+    own_ab.wait()
+
+    def low_tiles(first, count):
+        def body(i, _):
+            t = first + i
+            a_t = ab_all[tab[o_place + t]][:, :depth]
+            part[t] = lax.dot_general(a_t, x[t], NT, preferred_element_type=F32)
+            return 0
+        lax.fori_loop(0, count, body, 0)
+
+    def grad_slots():
+        def body(s, _):
+            b_s = ab_all[tab[o_splace + s]][:, depth:]
+            part[tiles + s] = lax.dot_general(b_s, dy[s], NT, preferred_element_type=F32)
+            return 0
+        lax.fori_loop(0, tiles, body, 0)
+
+    now = w_step(0)
+    flying += now
+    low_tiles(0, tiles)
+    for copy in now:
+        copy.wait_recv()
+
+    now = w_step(1)
+    flying += now
+    grad_slots()
+    part_copy = send(part, part_got, part_sem, (), {"mp": 1 - core})
+    for copy in now:
+        copy.wait_recv()
+
+    now = w_step(2)
+    flying += now
+    part_copy.wait()
+
+    def settle(t, _):
+        low[t] = (part[t] + part_got[t]).astype(BF16)
+        grad[t] = (SCALE * (part[tiles + t] + part_got[tiles + t])).astype(BF16)
+        return 0
+    lax.fori_loop(0, tiles, settle, 0)
+
+    def fill(r, _):
+        for l in range(2):
+            swap[4 * r + l] = low[tab[o_ltile + 2 * r + l]]
+            swap[4 * r + 2 + l] = grad[tab[o_lslot + 2 * r + l]]
+        return 0
+    lax.fori_loop(0, 8, fill, 0)
+    swaps = []
+    for d in range(1, 8):
+        to = lax.rem(me + d, 8)
+        swaps.append(send(swap.at[pl.ds(4 * to, 4)], swap_got.at[pl.ds(4 * me, 4)],
+                          swap_sem, (d,), {"dp": to}))
+    swap_got[pl.ds(4 * me, 4)] = swap[pl.ds(4 * me, 4)]
+    for copy in now:
+        copy.wait_recv()
+
+    now = w_step(3)
+    flying += now
+    for copy in swaps:
+        copy.wait()
+
+    def spread(index, keep, place):
+        for t in range(tiles):
+            value = swap_got[tab[index + t]]
+            home = jnp.where(tab[keep + t] > 0, tab[place + t], -1)
+            for p in range(16):
+                wide[pl.ds(32 * p, 32), pl.ds(ROWS * t, ROWS)] = jnp.where(home == p, value, zero)
+
+    spread(o_got, o_here, o_place)
+    for copy in now:
+        copy.wait_recv()
+
+    now = w_step(4)
+    flying += now
+
+    def a_sum(c, _):
+        at = pl.ds(pl.multiple_of(c * 512, 512), 512)
+        xs = x[:, :, at].reshape(tiles * ROWS, 512)
+        acc[:, :, at] = jnp.dot(wide[...], xs, preferred_element_type=F32).reshape(16, 32, 512)
+        return 0
+    lax.fori_loop(0, depth // 512, a_sum, 0)
+    for copy in now:
+        copy.wait_recv()
+
+    now = w_step(5)
+    flying += now
+    spread(o_slow, o_fill, o_splace)
+    acc[:, :, depth:] = SCALE * jnp.dot(
+        wide[...], dy[...].reshape(tiles * ROWS, cols), preferred_element_type=F32
+    ).reshape(16, 32, cols)
+    for copy in now:
+        copy.wait_recv()
+
+    now = w_step(6)
+    flying += now
+    for way in range(2):
+        owner = rank_at(pos - 1 if way == 0 else pos + 1)
+        rs_send[way, 0] = acc[2 * owner + way].astype(BF16)
+    for copy in now:
+        copy.wait_recv()
+    own_w.wait()
+
+    mine = pl.ds(pl.multiple_of(core * cols, cols), cols)
+    theirs = pl.ds(pl.multiple_of((1 - core) * cols, cols), cols)
+    halves = []
+
+    def project(k):
+        rows = x[pl.ds(2 * k, 2)].reshape(2 * ROWS, depth)
+        away = jnp.dot(rows, w_all[:, theirs], preferred_element_type=F32)
+        half_send[pl.ds(2 * k, 2)] = away.astype(BF16).reshape(2, ROWS, cols)
+        halves.append(send(half_send.at[pl.ds(2 * k, 2)], half_got.at[pl.ds(2 * k, 2)],
+                           half_sem, (k,), {"mp": 1 - core}))
+        home = jnp.dot(rows, w_all[:, mine], preferred_element_type=F32)
+        y[pl.ds(2 * k, 2)] = home.reshape(2, ROWS, cols)
+
+    pieces = tiles // 2
+    for s in range(7):
+        now = [send(rs_send.at[way, s], rs_got.at[way, s], rs_sem, (way, s), {"dp": hops[way]})
+               for way in range(2)]
+        flying += now
+        if s < pieces:
+            project(s)
+        for way in range(2):
+            now[way].wait_recv()
+            if s < 6:
+                owner = rank_at(pos - 2 - s if way == 0 else pos + 2 + s)
+                rs_send[way, s + 1] = (
+                    acc[2 * owner + way] + rs_got[way, s].astype(F32)
+                ).astype(BF16)
+            else:
+                grads[way] = acc[2 * me + way] + rs_got[way, s].astype(F32)
+
+    for copy in halves:
+        copy.wait()
+
+    def finish(t, _):
+        low_t = jnp.transpose(low[t].astype(F32)).astype(BF16)
+        b_t = ab_all[tab[o_place + t]][:, depth:]
+        adapted = jnp.dot(low_t, b_t, preferred_element_type=F32)
+        total = y[t] + SCALE * adapted + half_got[t].astype(F32)
+        half_send[t] = total.astype(BF16)
+        return 0
+    lax.fori_loop(0, tiles, finish, 0)
+
+    rows_out = []
+    for d in range(1, 8):
+        to = lax.rem(me + d, 8)
+        for l in range(2):
+            y_send[2 * to + l] = half_send[tab[o_ltile + 2 * to + l]]
+        rows_out.append(send(y_send.at[pl.ds(2 * to, 2)], y_got.at[pl.ds(2 * me, 2)],
+                             y_sem, (d,), {"dp": to}))
+    for l in range(2):
+        y_got[2 * me + l] = half_send[tab[o_ltile + 2 * me + l]]
+    for copy in flying:
+        copy.wait_send()
+    for copy in rows_out:
+        copy.wait()
+
+    def place_slot(s, _):
+        moved[s] = jnp.where(tab[o_fill + s] > 0, y_got[tab[o_sy + s]], zero)
+        return 0
+    lax.fori_loop(0, tiles, place_slot, 0)
+
+
+def pick(mask, values):
+    return jnp.sum(jnp.where(mask, values, 0), axis=-1)
+
+
+def on_grid(x, w, a, b, dy, target, tenant, storage):
+    ranks = lax.axis_size("dp")
+    me = lax.axis_index("dp")
+    tiles = x.shape[0] // ROWS
+    owned, depth, rank = a.shape
+    cols = dy.shape[1]
+    ids = jnp.arange(tenant.shape[0], dtype=jnp.int32)
+    place = pick(tenant[:, None] == jnp.arange(storage.shape[0])[None, :], storage[None, :])
+    dest = jnp.where(target >= 0, target // tiles, -1)
+    rank_of = ids // tiles
+    before = (
+        (rank_of[:, None] == rank_of[None, :])
+        & (dest[:, None] == dest[None, :])
+        & (ids[None, :] < ids[:, None])
+    )
+    level = jnp.minimum(jnp.sum(before.astype(jnp.int32), axis=1), 1)
+    mine = me * tiles + jnp.arange(tiles, dtype=jnp.int32)
+    at_mine = mine[:, None] == ids[None, :]
+    my_place = pick(at_mine, place[None, :])
+    my_dest = pick(at_mine, dest[None, :])
+    my_level = pick(at_mine, level[None, :])
+    here = (my_dest >= 0).astype(jnp.int32)
+    my_got = jnp.where(my_dest >= 0, 4 * my_dest + 2 + my_level, 0)
+    hit = target[None, :] == mine[:, None]
+    filled = jnp.sum(hit.astype(jnp.int32), axis=1)
+    s_place = pick(hit, place[None, :])
+    s_low = pick(hit, (4 * rank_of + level)[None, :])
+    s_row = pick(hit, (2 * rank_of + level)[None, :])
+    lanes = jnp.arange(2 * ranks, dtype=jnp.int32)
+    order = jnp.arange(tiles, dtype=jnp.int32)
+    t_lane = jnp.where(my_dest >= 0, 2 * my_dest + my_level, -1)
+    s_lane = jnp.where(filled > 0, s_row, -1)
+    lane_tile = pick(lanes[:, None] == t_lane[None, :], order[None, :])
+    lane_slot = pick(lanes[:, None] == s_lane[None, :], order[None, :])
+    table = jnp.concatenate(
+        [my_place, my_got, here, s_place, s_low, s_row, filled, lane_tile, lane_slot]
+    ).astype(jnp.int32)
+    ab = jnp.concatenate([a.transpose(0, 2, 1), b], axis=2)
+    wide = depth + cols
+    vmem = pl.BlockSpec(memory_space=pltpu.VMEM)
+    dma = pltpu.SemaphoreType.DMA
+    tile = (tiles, ROWS, cols)
+    moved, grads = pl.pallas_call(
+        kernel,
+        out_shape=(
+            jax.ShapeDtypeStruct(tile, BF16),
+            jax.ShapeDtypeStruct((owned, rank, wide), F32),
+        ),
+        in_specs=[pl.BlockSpec(memory_space=pltpu.SMEM)] + [vmem] * 4,
+        out_specs=(vmem, vmem),
+        scratch_shapes=[
+            pltpu.VMEM((depth, ranks * w.shape[1]), BF16),
+            pltpu.VMEM((ranks * owned, rank, wide), BF16),
+            pltpu.VMEM((ranks * owned * rank, tiles * ROWS), BF16),
+            pltpu.VMEM((ranks * owned, rank, wide), F32),
+            pltpu.VMEM((2 * tiles, rank, ROWS), F32),
+            pltpu.VMEM((2 * tiles, rank, ROWS), F32),
+            pltpu.VMEM((tiles, rank, ROWS), BF16),
+            pltpu.VMEM((tiles, rank, ROWS), BF16),
+            pltpu.VMEM((4 * ranks, rank, ROWS), BF16),
+            pltpu.VMEM((4 * ranks, rank, ROWS), BF16),
+            pltpu.VMEM((2, ranks - 1, rank, wide), BF16),
+            pltpu.VMEM((2, ranks - 1, rank, wide), BF16),
+            pltpu.VMEM(tile, BF16),
+            pltpu.VMEM(tile, BF16),
+            pltpu.VMEM(tile, F32),
+            pltpu.VMEM((2 * ranks, ROWS, cols), BF16),
+            pltpu.VMEM((2 * ranks, ROWS, cols), BF16),
+            dma((2,)),
+            dma((2, 2, ranks - 1)),
+            dma((2, 2, ranks - 1)),
+            dma((2,)),
+            dma((2, ranks)),
+            dma((2, 2, ranks - 1)),
+            dma((2, tiles // 2)),
+            dma((2, ranks)),
+        ],
+        compiler_params=pltpu.CompilerParams(
+            collective_id=0, has_side_effects=True, vmem_limit_bytes=60 * 1024 * 1024
+        ),
+    )(
+        table,
+        x.reshape(tiles, ROWS, depth),
+        w,
+        ab,
+        dy.reshape(tiles, ROWS, cols),
+    )
+    grad_a = grads[:, :, :depth].transpose(0, 2, 1)
+    return moved.reshape(tiles * ROWS, cols), grad_a, grads[:, :, depth:]
+
 
 def solution(mesh):
     return jax.shard_map(
-        on_device,
+        on_grid if mesh.shape["dp"] == 8 else on_device,
         mesh=mesh,
         in_specs=(
             P(("group", "dp"), "mp"),

time: 311 us -> 191 us (0.61)
  the two profiles are of different devices: /device:TPU:0 before, /device:TPU:12 now
where the time goes in v2:
time: 191 us; the launch traced here: 190 us
  Pallas kernels  178 us (93%)
  local copies, waits for them, and re-layouts  6.69 us (4%)
  other arithmetic  4.55 us (2%)
    pallas_call x1, Pallas kernels, on_grid(): pl.pallas_call(kernel, out_shape=(jax.ShapeDtypeStruct(tile, BF16), jax.S...  178 us

profile of v2, /device:TPU:12, one launch (start us, length us, event | category | flops | bytes accessed | tf_op | source)
XLA Modules:
  0.0 190.3 jit_solution(1973152850538069211)
XLA Ops:
  0.6 0.8 select_reduce_fusion.5
  1.4 0.7 and_select_fusion
  2.1 0.2 convert_reduce_fusion
  2.3 0.9 fusion.4
  3.2 0.1 select_reduce_fusion
  3.4 0.1 select_reduce_fusion.1
  3.5 0.6 concatenate.6.tab
  4.1 1.7 pad_maximum_fusion.ab
  5.8 178.4 %shard_map.103 = (bf16[12,128,512]{2,1,0:T(8,128)(2,1)}, f32[2,32,2560]{2,1,0:T(8,128)}) custom-call(s32[116]{0:T(128)} %concatenate.6.tab, bf16[12,128,2048]{2,1,0:T(8,128)(2,1)} %bitcast.6, bf16[2048,128]{1,0:T(8,128)(2,1)} %w.1, bf16[2,32,2560]{2,1,0:T(8,128)(2,1)} %pad_maximum_fusion.ab, bf16[12,128,512]{2,1,0:T(8,128)(2,1)} %bitcast.8), custom_call_target="tpu_custom_call" | custom-call | tf_op jit(solution)/shard_map/pallas_call | solution.py:400
  184.2 1.6 slice.7
  185.8 1.9 slice_bitcast_fusion
  187.6 2.7 %copy.12 = bf16[1536,512]{1,0:T(8,128)(2,1)} copy(bf16[1536,512]{1,0:T(8,128)(2,1)} %bitcast.7) | data formatting | bytes 3145728
  (5 shorter events, 0.0 us)

commit v3 on v2

--- a/solution.py
+++ b/solution.py
@@ -119,17 +119,18 @@
 
 
 def kernel(
-    tab, x, w, ab, dy,
-    moved, grads,
+    tab, x, w, a, b, dy,
+    moved, grad_a, grad_b,
     w_all, ab_all, wide, acc, part, part_got, low, grad, swap, swap_got,
     rs_send, rs_got, half_send, half_got, y, y_send, y_got,
-    own_sem, ab_sem, w_sem, part_sem, swap_sem, rs_sem, half_sem, y_sem,
+    own_sem, ab_sem, w_sem, x_sem, part_sem, swap_sem, rs_sem, half_sem, y_sem,
 ):
     tiles, _, depth = x.shape
     cols = dy.shape[2]
     wcols = w.shape[1]
     me = lax.axis_index("dp")
     core = lax.axis_index("mp")
+    group = lax.axis_index("group")
     z, side = me // 2, me % 2
     pos = jnp.where(side == 0, z, 7 - z)
     hops = (rank_at(pos + 1), rank_at(pos - 1))
@@ -147,11 +148,17 @@
         copy.start()
         return copy
 
-    own_ab = pltpu.make_async_copy(ab, ab_all.at[pl.ds(2 * me, 2)], own_sem.at[0])
+    own_a = pltpu.make_async_copy(
+        a, ab_all.at[pl.ds(2 * me, 2), :, pl.ds(0, depth)], own_sem.at[0]
+    )
+    own_b = pltpu.make_async_copy(
+        b, ab_all.at[pl.ds(2 * me, 2), :, pl.ds(depth, cols)], own_sem.at[2]
+    )
     own_w = pltpu.make_async_copy(
         w, w_all.at[:, pl.ds(pl.multiple_of(me * wcols, wcols), wcols)], own_sem.at[1]
     )
-    own_ab.start()
+    own_a.start()
+    own_b.start()
     own_w.start()
 
     barrier = pltpu.get_barrier_semaphore()
@@ -160,35 +167,65 @@
             barrier, inc=1, device_id={"dp": lax.rem(me + d, 8)}, device_id_type=MESH
         )
     pl.semaphore_signal(barrier, inc=1, device_id={"mp": 1 - core}, device_id_type=MESH)
-    pl.semaphore_wait(barrier, 8)
+    pl.semaphore_signal(barrier, inc=1, device_id={"group": 1 - group}, device_id_type=MESH)
+    pl.semaphore_wait(barrier, 9)
 
     def ab_step(s):
         out = []
         for way in range(2):
             owner = rank_at(pos - s if way == 0 else pos + s)
             where = ab_all.at[2 * owner + way]
-            out.append(send(ab.at[way] if s == 0 else where, where, ab_sem, (way, s),
+            out.append(send(where, where, ab_sem, (way, s),
                             {"dp": hops[way]}))
         return out
 
+    ring = depth * 11 // 16
+    crossing = depth - ring
+    ring_from = pl.multiple_of(jnp.where(group == 0, crossing, 0), 64)
+    cross_from = pl.multiple_of(jnp.where(group == 0, ring, 0), 64)
+
+    def column(owner):
+        return pl.ds(pl.multiple_of(owner * wcols, wcols), wcols)
+
     def w_step(s):
         out = []
-        rows = depth // 2
+        rows = ring // 2
         for way in range(2):
             owner = rank_at(pos - s if way == 0 else pos + s)
-            there = pl.ds(pl.multiple_of(owner * wcols, wcols), wcols)
-            where = w_all.at[pl.ds(way * rows, rows), there]
-            out.append(send(w.at[pl.ds(way * rows, rows)] if s == 0 else where, where,
+            here = pl.ds(pl.multiple_of(ring_from + way * rows, 64), rows)
+            where = w_all.at[here, column(owner)]
+            out.append(send(w.at[here] if s == 0 else where, where,
                             w_sem, (way, s), {"dp": hops[way]}))
         return out
 
+    def w_arrive(s, copies):
+        for copy in copies:
+            copy.wait_recv()
+        owner = rank_at(jnp.where(group == 0, pos + 1 + s, pos - 1 - s))
+        where = w_all.at[pl.ds(cross_from, crossing), column(owner)]
+        return send(where, where, x_sem, (s,), {"group": 1 - group})
+
     flying = []
+    crossings = []
+    own_a.wait()
+    own_b.wait()
+    w_now = None
     for s in range(7):
         now = ab_step(s)
         flying += now
+        if s % 2 == 0 and s < 6:
+            if s > 0:
+                crossings.append(w_arrive(s // 2 - 1, w_now))
+            w_now = w_step(s // 2)
+            flying += w_now
         for copy in now:
             copy.wait_recv()
-    own_ab.wait()
+
+    def w_next(s):
+        crossings.append(w_arrive(s - 1, w_now))
+        copies = w_step(s)
+        flying.extend(copies)
+        return copies
 
     def low_tiles(first, count):
         def body(i, _):
@@ -205,21 +242,12 @@
             return 0
         lax.fori_loop(0, tiles, body, 0)
 
-    now = w_step(0)
-    flying += now
-    low_tiles(0, tiles)
-    for copy in now:
-        copy.wait_recv()
-
-    now = w_step(1)
-    flying += now
+    low_tiles(0, tiles // 2)
+    w_now = w_next(3)
+    low_tiles(tiles // 2, tiles - tiles // 2)
     grad_slots()
     part_copy = send(part, part_got, part_sem, (), {"mp": 1 - core})
-    for copy in now:
-        copy.wait_recv()
-
-    now = w_step(2)
-    flying += now
+    w_now = w_next(4)
     part_copy.wait()
 
     def settle(t, _):
@@ -240,11 +268,6 @@
         swaps.append(send(swap.at[pl.ds(4 * to, 4)], swap_got.at[pl.ds(4 * me, 4)],
                           swap_sem, (d,), {"dp": to}))
     swap_got[pl.ds(4 * me, 4)] = swap[pl.ds(4 * me, 4)]
-    for copy in now:
-        copy.wait_recv()
-
-    now = w_step(3)
-    flying += now
     for copy in swaps:
         copy.wait()
 
@@ -256,11 +279,7 @@
                 wide[pl.ds(32 * p, 32), pl.ds(ROWS * t, ROWS)] = jnp.where(home == p, value, zero)
 
     spread(o_got, o_here, o_place)
-    for copy in now:
-        copy.wait_recv()
-
-    now = w_step(4)
-    flying += now
+    w_now = w_next(5)
 
     def a_sum(c, _):
         at = pl.ds(pl.multiple_of(c * 512, 512), 512)
@@ -268,56 +287,68 @@
         acc[:, :, at] = jnp.dot(wide[...], xs, preferred_element_type=F32).reshape(16, 32, 512)
         return 0
     lax.fori_loop(0, depth // 512, a_sum, 0)
-    for copy in now:
-        copy.wait_recv()
-
-    now = w_step(5)
-    flying += now
+    w_now = w_next(6)
     spread(o_slow, o_fill, o_splace)
     acc[:, :, depth:] = SCALE * jnp.dot(
         wide[...], dy[...].reshape(tiles * ROWS, cols), preferred_element_type=F32
     ).reshape(16, 32, cols)
-    for copy in now:
-        copy.wait_recv()
-
-    now = w_step(6)
-    flying += now
-    for way in range(2):
-        owner = rank_at(pos - 1 if way == 0 else pos + 1)
-        rs_send[way, 0] = acc[2 * owner + way].astype(BF16)
-    for copy in now:
-        copy.wait_recv()
+    block = (depth + cols) // 2
+    rs_now = {}
+
+    def rs_store(s, way, c, value):
+        rs_send[way, s, c] = value
+        rs_now[s, way, c] = send(rs_send.at[way, s, c], rs_got.at[way, s, c],
+                                 rs_sem, (way, s, c), {"dp": hops[way]})
+        flying.append(rs_now[s, way, c])
+
+    def rs_advance(s, c):
+        at = pl.ds(c * block, block)
+        for way in range(2):
+            rs_now[s, way, c].wait_recv()
+            got = rs_got[way, s, c].astype(F32)
+            if s < 6:
+                owner = rank_at(pos - 2 - s if way == 0 else pos + 2 + s)
+                rs_store(s + 1, way, c, (acc[2 * owner + way, :, at] + got).astype(BF16))
+            else:
+                total = acc[2 * me + way, :, at] + got
+                if c == 0:
+                    grad_a[way, :, pl.ds(0, block)] = total
+                else:
+                    grad_a[way, :, pl.ds(block, depth - block)] = total[:, : depth - block]
+                    grad_b[way] = total[:, depth - block :]
+
+    for c in range(2):
+        for way in range(2):
+            owner = rank_at(pos - 1 if way == 0 else pos + 1)
+            rs_store(0, way, c, acc[2 * owner + way, :, pl.ds(c * block, block)].astype(BF16))
+    crossings.append(w_arrive(6, w_now))
     own_w.wait()
+    rs_advance(0, 0)
+    rs_advance(0, 1)
+    for copy in crossings:
+        copy.wait()
 
     mine = pl.ds(pl.multiple_of(core * cols, cols), cols)
     theirs = pl.ds(pl.multiple_of((1 - core) * cols, cols), cols)
     halves = []
 
-    def project(k):
+    def project(k, part_of):
         rows = x[pl.ds(2 * k, 2)].reshape(2 * ROWS, depth)
-        away = jnp.dot(rows, w_all[:, theirs], preferred_element_type=F32)
-        half_send[pl.ds(2 * k, 2)] = away.astype(BF16).reshape(2, ROWS, cols)
-        halves.append(send(half_send.at[pl.ds(2 * k, 2)], half_got.at[pl.ds(2 * k, 2)],
-                           half_sem, (k,), {"mp": 1 - core}))
-        home = jnp.dot(rows, w_all[:, mine], preferred_element_type=F32)
-        y[pl.ds(2 * k, 2)] = home.reshape(2, ROWS, cols)
-
-    pieces = tiles // 2
-    for s in range(7):
-        now = [send(rs_send.at[way, s], rs_got.at[way, s], rs_sem, (way, s), {"dp": hops[way]})
-               for way in range(2)]
-        flying += now
-        if s < pieces:
-            project(s)
-        for way in range(2):
-            now[way].wait_recv()
-            if s < 6:
-                owner = rank_at(pos - 2 - s if way == 0 else pos + 2 + s)
-                rs_send[way, s + 1] = (
-                    acc[2 * owner + way] + rs_got[way, s].astype(F32)
-                ).astype(BF16)
-            else:
-                grads[way] = acc[2 * me + way] + rs_got[way, s].astype(F32)
+        if part_of == 0:
+            away = jnp.dot(rows, w_all[:, theirs], preferred_element_type=F32)
+            half_send[pl.ds(2 * k, 2)] = away.astype(BF16).reshape(2, ROWS, cols)
+            halves.append(send(half_send.at[pl.ds(2 * k, 2)], half_got.at[pl.ds(2 * k, 2)],
+                               half_sem, (k,), {"mp": 1 - core}))
+        else:
+            home = jnp.dot(rows, w_all[:, mine], preferred_element_type=F32)
+            y[pl.ds(2 * k, 2)] = home.reshape(2, ROWS, cols)
+
+    todo = [(s, c) for s in range(1, 7) for c in range(2)]
+    for part_of in range(2):
+        for k in range(tiles // 2):
+            project(k, part_of)
+            if k % 2 == 1:
+                rs_advance(*todo.pop(0))
 
     for copy in halves:
         copy.wait()
@@ -340,6 +371,8 @@
                              y_sem, (d,), {"dp": to}))
     for l in range(2):
         y_got[2 * me + l] = half_send[tab[o_ltile + 2 * me + l]]
+    for s, c in todo:
+        rs_advance(s, c)
     for copy in flying:
         copy.wait_send()
     for copy in rows_out:
@@ -392,19 +425,19 @@
     table = jnp.concatenate(
         [my_place, my_got, here, s_place, s_low, s_row, filled, lane_tile, lane_slot]
     ).astype(jnp.int32)
-    ab = jnp.concatenate([a.transpose(0, 2, 1), b], axis=2)
     wide = depth + cols
     vmem = pl.BlockSpec(memory_space=pltpu.VMEM)
     dma = pltpu.SemaphoreType.DMA
     tile = (tiles, ROWS, cols)
-    moved, grads = pl.pallas_call(
+    moved, grad_a, grad_b = pl.pallas_call(
         kernel,
         out_shape=(
             jax.ShapeDtypeStruct(tile, BF16),
-            jax.ShapeDtypeStruct((owned, rank, wide), F32),
+            jax.ShapeDtypeStruct((owned, rank, depth), F32),
+            jax.ShapeDtypeStruct((owned, rank, cols), F32),
         ),
-        in_specs=[pl.BlockSpec(memory_space=pltpu.SMEM)] + [vmem] * 4,
-        out_specs=(vmem, vmem),
+        in_specs=[pl.BlockSpec(memory_space=pltpu.SMEM)] + [vmem] * 5,
+        out_specs=(vmem, vmem, vmem),
         scratch_shapes=[
             pltpu.VMEM((depth, ranks * w.shape[1]), BF16),
             pltpu.VMEM((ranks * owned, rank, wide), BF16),
@@ -416,19 +449,20 @@
             pltpu.VMEM((tiles, rank, ROWS), BF16),
             pltpu.VMEM((4 * ranks, rank, ROWS), BF16),
             pltpu.VMEM((4 * ranks, rank, ROWS), BF16),
-            pltpu.VMEM((2, ranks - 1, rank, wide), BF16),
-            pltpu.VMEM((2, ranks - 1, rank, wide), BF16),
+            pltpu.VMEM((2, ranks - 1, 2, rank, wide // 2), BF16),
+            pltpu.VMEM((2, ranks - 1, 2, rank, wide // 2), BF16),
             pltpu.VMEM(tile, BF16),
             pltpu.VMEM(tile, BF16),
             pltpu.VMEM(tile, F32),
             pltpu.VMEM((2 * ranks, ROWS, cols), BF16),
             pltpu.VMEM((2 * ranks, ROWS, cols), BF16),
-            dma((2,)),
+            dma((3,)),
             dma((2, 2, ranks - 1)),
             dma((2, 2, ranks - 1)),
+            dma((2, ranks - 1)),
             dma((2,)),
             dma((2, ranks)),
-            dma((2, 2, ranks - 1)),
+            dma((2, 2, ranks - 1, 2)),
             dma((2, tiles // 2)),
             dma((2, ranks)),
         ],
@@ -439,16 +473,16 @@
         table,
         x.reshape(tiles, ROWS, depth),
         w,
-        ab,
+        a.transpose(0, 2, 1),
+        b,
         dy.reshape(tiles, ROWS, cols),
     )
-    grad_a = grads[:, :, :depth].transpose(0, 2, 1)
-    return moved.reshape(tiles * ROWS, cols), grad_a, grads[:, :, depth:]
+    return moved.reshape(tiles * ROWS, cols), grad_a.transpose(0, 2, 1), grad_b
 
 
 def solution(mesh):
     return jax.shard_map(
-        on_grid if mesh.shape["dp"] == 8 else on_device,
+        on_grid if (mesh.shape["dp"], mesh.shape["group"]) == (8, 2) else on_device,
         mesh=mesh,
         in_specs=(
             P(("group", "dp"), "mp"),

time: 191 us -> 162 us (0.85)
  the two profiles are of different devices: /device:TPU:12 before, /device:TPU:0 now
where the time goes in v3:
time: 162 us
  Pallas kernels  154 us (95%)
  local copies, waits for them, and re-layouts  4.77 us (3%)
  other arithmetic  2.81 us (2%)
    pallas_call x1, Pallas kernels, on_grid(): pl.pallas_call(kernel, out_shape=(jax.ShapeDtypeStruct(tile, BF16), jax.S...  154 us
    unnamed x7, local copies, waits for them, and re-layouts  4.17 us

profile of v3, /device:TPU:0, one launch (start us, length us, event | category | flops | bytes accessed | tf_op | source)
XLA Modules:
  0.0 162.3 jit_solution(14548745826299279497)
XLA Ops:
  0.6 0.8 select_reduce_fusion.5
  1.4 0.7 and_select_fusion
  2.1 0.2 convert_reduce_fusion
  2.3 0.9 fusion.4
  3.2 0.1 select_reduce_fusion
  3.4 0.1 select_reduce_fusion.1
  3.5 0.6 concatenate.3.tab
  4.1 154.0 %shard_map.103 = (bf16[12,128,512]{2,1,0:T(8,128)(2,1)}, f32[2,32,2048]{2,1,0:T(8,128)}, f32[2,32,512]{2,1,0:T(8,128)}) custom-call(s32[116]{0:T(128)} %concatenate.3.tab, bf16[12,128,2048]{2,1,0:T(8,128)(2,1)} %bitcast.5, bf16[2048,128]{1,0:T(8,128)(2,1)} %w.1, bf16[2,32,2048]{2,1,0:T(8,128)(2,1)} %bitcast.9, bf16[2,32,512]{2,1,0:T(8,128)(2,1)} %b.1, ...), custom_call_target="tpu_custom_call" | custom-call | tf_op jit(solution)/shard_map/pallas_call | solution.py:432
  158.1 0.0 copy-start
  158.1 0.0 copy-start.1
  158.1 2.7 %copy.14 = bf16[1536,512]{1,0:T(8,128)(2,1)} copy(bf16[1536,512]{1,0:T(8,128)(2,1)} %bitcast.6) | data formatting | bytes 3145728
  160.8 0.0 copy-done
  160.8 0.8 copy.15
  161.6 0.0 copy-done.1
  161.6 0.7 copy.16
  (5 shorter events, 0.0 us)
Async XLA Ops:
  158.1 2.7 %copy-start = (f32[2,32,2048]{2,1,0:T(8,128)S(1)}, f32[2,32,2048]{2,1,0:T(8,128)}, u32[]{:S(2)}) copy-start(f32[2,32,2048]{2,1,0:T(8,128)} %get-tuple-element.7) | copy-start | bytes 1572868
  158.1 3.5 %copy-start.1 = (f32[2,32,512]{2,1,0:T(8,128)S(1)}, f32[2,32,512]{2,1,0:T(8,128)}, u32[]{:S(2)}) copy-start(f32[2,32,512]{2,1,0:T(8,128)} %get-tuple-element.28) | copy-start | bytes 393220
